TPU v7x, 32 devices: a whole 2x2x4 slice. The times are simulated.
32 devices in a mesh: groups: 1, pair: 8 (over z, core), vir: 4 (over y, x).
Axes of the slice: x: 2, y: 2, z: 4, core: 2. Of those that a mesh axis runs over, the one named last changes fastest.
Arguments:
- amplitudes: bfloat16 [8, 2560, 2560], P(('groups', 'pair'), 'vir'), may hold values from -6 to 6
- ladder_factor: bfloat16 [1, 20, 4, 128, 128], P('groups'), may hold values from -0.25 to 0.25
- ladder_tiles: int32 [20, 4], P('groups'), may hold values from 0 to 19, as said below
- cycle_integrals: bfloat16 [80, 4, 128, 128], P(('groups', 'pair')), may hold values from -0.25 to 0.25
- cycle_tiles: int32 [80, 4], P('groups'), may hold values from 0 to 79, as said below
- cycle_slots: int32 [80], P('groups'), may hold values from 0 to 79, as said below
- slab_order: int32 [8], P('groups'), may hold values from 0 to 7, each once
- amp_mask: int32 [8, 20, 20], P(('groups', 'pair'), 'vir'), may hold values 0 or 1
Outputs:
- residual: bfloat16 [8, 2560, 2560], P(('groups', 'pair'), 'vir')
Inputs may be any that keep to these rules, and one draw needn't show every extreme that they name: `ladder_tiles`: row t names 4 different tiles, the first of them t itself. `cycle_tiles`: row t names 4 different tiles, the first of them t itself. `cycle_slots`: different column tiles have different slots.
All inputs are finite; a program needn't handle non-finite values. No bound on the sum of `amp_mask` on one device may be relied on, other than what follows from the above.
Results may differ from a plain program's by a relative error of at most 0.0051.
Values may be sent and summed in bfloat16 or wider, within the bound.
A program may use at most 192 MiB of HBM per device.

v0:
```python
import jax
import jax.numpy as jnp
from jax import lax
from jax.sharding import PartitionSpec as P

NJ = 4


def on_device(
    amplitudes,
    ladder_factor,
    ladder_tiles,
    cycle_integrals,
    cycle_tiles,
    cycle_slots,
    slab_order,
    amp_mask,
):
    tile_size = ladder_factor.shape[-1]
    row_count = amplitudes.shape[1]
    full_width = amplitudes.shape[2]
    tile_count = full_width // tile_size
    local_tiles = row_count // tile_size
    first_tile = lax.axis_index("vir") * local_tiles
    own_rows = lax.dynamic_slice_in_dim(ladder_tiles, first_tile, local_tiles, 0)
    gathered = lax.all_gather(amplitudes[0], "vir", axis=0, tiled=True)
    picked = jnp.take(
        gathered.reshape(tile_count, tile_size, tile_count, tile_size), own_rows, axis=0
    )
    factor = ladder_factor[0]
    own_factor = lax.dynamic_slice_in_dim(factor, first_tile, local_tiles, 0)
    inner_term = jnp.einsum(
        "tkac,tkcsd->stad", own_factor, picked, preferred_element_type=jnp.float32
    ).astype(jnp.bfloat16)
    inner_term = inner_term.reshape(tile_count, row_count, tile_size)
    chosen = jnp.take(inner_term, ladder_tiles, axis=0)
    ladder_sum = jnp.einsum("rkad,rkbd->rab", chosen, factor, preferred_element_type=jnp.float32)
    exchanged = lax.all_to_all(amplitudes, "pair", split_axis=1, concat_axis=0, tiled=True)
    pair_count = exchanged.shape[0]
    sub_rows = exchanged.shape[1]
    outer_count = pair_count // NJ
    positions = jnp.arange(pair_count, dtype=jnp.int32)
    inverse = jnp.zeros((pair_count,), jnp.int32).at[slab_order].set(positions)
    pair_grid = jnp.take(exchanged, inverse, axis=0)
    col_tiles = NJ * tile_count
    left_tiles = (
        pair_grid.reshape(outer_count, NJ, sub_rows, tile_count, tile_size)
        .transpose(1, 3, 2, 0, 4)
        .reshape(col_tiles, sub_rows * outer_count, tile_size)
    )
    slot_tiles = lax.all_gather(cycle_integrals, "pair", axis=0, tiled=True)
    integrals = jnp.take(slot_tiles, cycle_slots, axis=0)
    columns = jnp.take(left_tiles, cycle_tiles, axis=0)
    cycle_term = jnp.einsum(
        "tkrc,tkcb->trb", columns, integrals, preferred_element_type=jnp.float32
    ).astype(jnp.bfloat16)
    cycle_back = (
        cycle_term.reshape(NJ, tile_count, sub_rows, outer_count, tile_size)
        .transpose(3, 0, 2, 1, 4)
        .reshape(pair_count, sub_rows, full_width)
    )
    cycle_back = jnp.take(cycle_back, slab_order, axis=0)
    returned = lax.all_to_all(cycle_back, "pair", split_axis=0, concat_axis=1, tiled=True)
    summed = ladder_sum.transpose(1, 0, 2).reshape(row_count, full_width) + returned[0].astype(
        jnp.float32
    )
    mask_tiles = amp_mask[0].astype(jnp.float32)[:, None, :, None]
    masked = summed.reshape(local_tiles, tile_size, tile_count, tile_size) * mask_tiles
    return masked.reshape(1, row_count, full_width).astype(jnp.bfloat16)


def solution(mesh):
    placed = (
        P(("groups", "pair"), "vir", None),
        P("groups", None, None, None, None),
        P("groups", None),
        P(("groups", "pair"), None, None, None),
        P("groups", None),
        P("groups"),
        P("groups"),
        P(("groups", "pair"), "vir", None),
    )
    return jax.shard_map(
        on_device,
        mesh=mesh,
        in_specs=placed,
        out_specs=P(("groups", "pair"), "vir", None),
        check_vma=False,
    )
```

profile of v0, /device:TPU:1, one launch (start us, length us, event | category | flops | bytes accessed | tf_op | source)
XLA Modules:
  0.0 384.8 jit_solution(5591474268174198279)
XLA Ops:
  6.5 0.0 copy-start
  6.5 0.7 all-gather.4.cloned.1.call-update
  7.3 0.0 all-gather.6.cloned.1.call-start
  7.3 0.7 all-gather.6.cloned.1.call-update
  8.0 16.4 %copy.68 = bf16[1,640,2560]{2,0,1:T(2,128)(2,1)} copy(bf16[1,640,2560]{2,1,0:T(8,128)(2,1)} %param.10) | data formatting | bytes 6553600 | tf_op args[0]
  24.4 0.5 broadcast.93
  25.0 71.4 %reduce = bf16[640,2560]{1,0:T(8,128)(2,1)} reduce(bf16[640,1,2560]{2,1,0:T(2,128)(2,1)} %bitcast.52, bf16[]{:T(256)} %broadcast.93), dimensions={1}, to_apply=%bitcast.48.reduce_sub_computation | reduce | bytes 6553602
  96.4 7.2 %reshape.190 = bf16[8,2,102400]{2,1,0:T(2,128)(2,1)} reshape(bf16[640,2560]{1,0:T(8,128)(2,1)} %reduce) | data formatting | bytes 6553600
  103.6 6.4 %all-to-all-start = ((bf16[8,2,102400]{2,1,0:T(2,128)(2,1)}), bf16[8,2,102400]{2,1,0:T(2,128)(2,1)}, u32[]{:S(2)}, u32[]{:S(2)}) async-start(bf16[8,2,102400]{2,1,0:T(2,128)(2,1)} %reshape.190), calls=%async_computation | async-start | bytes 6553600 | tf_op jit(solution)/shard_map/all_to_all | solution.py:38
  110.0 0.1 copy.53
  110.1 0.1 reshape.146
  110.2 0.1 copy.50
  110.4 0.8 scatter_custom_fusion
  111.3 72.3 %all-to-all-done = bf16[8,2,102400]{2,1,0:T(2,128)(2,1)} async-done(((bf16[8,2,102400]{2,1,0:T(2,128)(2,1)}), bf16[8,2,102400]{2,1,0:T(2,128)(2,1)}, u32[]{:S(2)}, u32[]{:S(2)}) %all-to-all-start) | async-done | bytes 3276832 | tf_op jit(solution)/shard_map/all_to_all | solution.py:38
  183.6 7.9 %reshape.191 = bf16[640,1,2560]{2,1,0:T(2,128)(2,1)} reshape(bf16[8,2,102400]{2,1,0:T(2,128)(2,1)} %all-to-all-done) | data formatting | bytes 6553600
  191.5 5.3 %copy.61 = bf16[1,640,2560]{2,1,0:T(8,128)(2,1)} copy(bf16[1,640,2560]{2,0,1:T(2,128)(2,1)} %bitcast.53) | data formatting | bytes 6553600
  196.8 4.4 %gather_fusion.4 = bf16[8,80,2560]{2,1,0:T(8,128)(2,1)} fusion(bf16[8,80,2560]{2,1,0:T(8,128)(2,1)} %bitcast.59, s32[1024]{0:T(1024)S(1)} %pad_clamp_fusion.3), kind=kCustom, calls=%fused_computation.clone | custom fusion | bytes 6553632 | tf_op jit(solution)/shard_map/jit(_take)/gather | solution.py:44
  201.2 4.0 %broadcast_select_fusion.1 = bf16[8,80,2560]{2,1,0:T(8,128)(2,1)} fusion(bf16[8,80,2560]{2,1,0:T(8,128)(2,1)} %gather_fusion.4, pred[8]{0:T(512)(128)(4,1)S(1)} %get-tuple-element.9), kind=kLoop, calls=%fused_computation.30 | loop fusion | flops 1638400 | bytes 6553608 | tf_op jit(solution)/shard_map/jit(_take)/select_n | solution.py:44
  205.2 6.8 %reshape.107 = bf16[2,4,80,20,128]{4,3,2,1,0:T(8,128)(2,1)} reshape(bf16[8,80,2560]{2,1,0:T(8,128)(2,1)} %broadcast_select_fusion.1) | data formatting | bytes 6553600 | tf_op jit(solution)/shard_map/reshape | solution.py:47
  212.0 7.2 %copy.52 = bf16[4,20,80,2,128]{4,3,2,1,0:T(2,128)(2,1)} copy(bf16[4,20,80,2,128]{4,1,2,0,3:T(8,128)(2,1)} %bitcast.54) | data formatting | bytes 6553600 | tf_op jit(solution)/shard_map/transpose | solution.py:48
  219.2 13.8 %gather_fusion.2 = bf16[320,160,128]{2,1,0:T(8,128)(2,1)} fusion(bf16[80,160,128]{2,1,0:T(8,128)(2,1)} %bitcast.50, s32[1024]{0:T(1024)S(1)} %pad_clamp_fusion.2), kind=kCustom, calls=%fused_computation.4 | custom fusion | bytes 26215680 | tf_op jit(solution)/shard_map/jit(_take)/gather | solution.py:53
  233.0 10.1 %gather_fusion.3 = bf16[80,4,128,128]{3,2,1,0:T(8,128)(2,1)} fusion(bf16[80,4,128,128]{3,2,1,0:T(8,128)(2,1)} %all-gather.4.cloned.1.call-done, s32[1024]{0:T(1024)S(1)} %pad_clamp_fusion.1), kind=kCustom, calls=%fused_computation.5 | custom fusion | bytes 20971840 | tf_op jit(solution)/shard_map/jit(_take)/gather | solution.py:52
  243.1 9.9 %bitcast_convert_fusion.1 = bf16[80,160,128]{2,1,0:T(8,128)(2,1)S(1)} fusion(bf16[80,4,128,128]{3,2,1,0:T(8,128)(2,1)} %gather_fusion.3, pred[80]{0:T(512)(128)(4,1)S(1)} %compare_and_fusion.2, bf16[80,4,160,128]{3,2,1,0:T(8,128)(2,1)} %bitcast.57, pred[80,4]{1,0:T(8,128)(4,1)S(1)} %copy.50), kind=kOutput, calls=%fused_computation.22 | convolution fusion | flops 1691156480 | bytes 26870160 | tf_op jit(solution)/shard_map/tkrc,tkcb->trb/dot_general | solution.py:54
  253.1 3.2 copy.67
  256.3 6.8 %reshape.110 = bf16[8,80,2560]{2,1,0:T(8,128)(2,1)} reshape(bf16[2,4,80,20,128]{4,3,2,1,0:T(8,128)(2,1)} %bitcast.55) | data formatting | bytes 6553600 | tf_op jit(solution)/shard_map/reshape | solution.py:60
  263.0 4.4 %gather_fusion.5 = bf16[8,80,2560]{2,1,0:T(8,128)(2,1)} fusion(bf16[8,80,2560]{2,1,0:T(8,128)(2,1)} %reshape.110, s32[1024]{0:T(1024)S(1)} %pad_clamp_fusion), kind=kCustom, calls=%fused_computation.1.clone | custom fusion | bytes 6553632 | tf_op jit(solution)/shard_map/jit(_take)/gather | solution.py:62
  267.4 4.0 %broadcast_select_fusion = bf16[8,80,2560]{2,1,0:T(8,128)(2,1)} fusion(bf16[8,80,2560]{2,1,0:T(8,128)(2,1)} %gather_fusion.5, pred[8]{0:T(512)(128)(4,1)S(1)} %get-tuple-element.8), kind=kLoop, calls=%fused_computation.29 | loop fusion | flops 1638400 | bytes 6553608 | tf_op jit(solution)/shard_map/jit(_take)/select_n | solution.py:62
  271.5 5.2 %all-to-all-start.1 = ((bf16[8,80,2560]{2,1,0:T(8,128)(2,1)}), bf16[8,80,2560]{2,1,0:T(8,128)(2,1)}, u32[]{:S(2)}, u32[]{:S(2)}) async-start(bf16[8,80,2560]{2,1,0:T(8,128)(2,1)} %broadcast_select_fusion), calls=%async_computation.1 | async-start | bytes 6553600 | tf_op jit(solution)/shard_map/all_to_all | solution.py:63
  276.7 3.6 mul.22
  280.3 8.6 %mul.23 = f32[1,640,2560]{2,1,0:T(8,128)} reshape(f32[5,128,20,128]{3,2,1,0:T(8,128)} %mul.22) | data formatting | bytes 13107200 | tf_op jit(solution)/shard_map/mul | solution.py:68
  288.9 0.1 compare_and_fusion.4
  289.0 0.1 copy.45
  289.1 0.1 reshape.130
  289.1 0.1 copy.44
  289.2 0.1 copy.49
  289.3 0.1 reshape.138
  289.5 0.1 copy.43
  289.6 0.0 all-gather.6.cloned.1.call-done
  289.6 22.8 %reshape.104 = bf16[20,128,20,128]{3,2,1,0:T(8,128)(2,1)} reshape(bf16[1,2560,2560]{2,1,0:T(8,128)(2,1)} %all-gather.6.cloned.1.call-done) | data formatting | bytes 26214400 | tf_op jit(solution)/shard_map/reshape | solution.py:28
  312.4 12.9 %gather_fusion = bf16[20,128,20,128]{3,2,1,0:T(8,128)(2,1)} fusion(bf16[20,128,20,128]{3,2,1,0:T(8,128)(2,1)} %reshape.104, s32[1024]{0:T(1024)S(1)} %pad_clamp_fusion.5), kind=kCustom, calls=%fused_computation.2 | custom fusion | bytes 26214480 | tf_op jit(solution)/shard_map/jit(_take)/gather | solution.py:27
  325.3 8.7 %copy.46 = bf16[20,128,20,128]{3,1,2,0:T(8,128)(2,1)S(1)} copy(bf16[20,128,20,128]{3,2,1,0:T(8,128)(2,1)} %gather_fusion) | data formatting | bytes 26214400 | tf_op jit(solution)/shard_map/jit(_take)/gather | solution.py:27
  334.1 4.4 %fusion.17 = bf16[20,5,128,128]{3,2,0,1:T(8,128)(2,1)} fusion(bf16[5,4,128,20,128]{4,2,3,1,0:T(8,128)(2,1)S(1)} %bitcast.56, pred[5,4]{1,0:T(8,128)(4,1)S(1)} %copy.44, bf16[1,20,4,128,128]{4,3,2,1,0:T(8,128)(2,1)S(1)} %copy-done, s32[]{:T(128)S(6)} %select_n.51), kind=kOutput, calls=%fused_computation.28 | convolution fusion | flops 1685913600 | bytes 17040388 | tf_op jit(solution)/shard_map/tkac,tkcsd->stad/dot_general | solution.py:32
  338.5 4.0 %copy.48 = bf16[20,5,128,128]{3,2,1,0:T(8,128)(2,1)} copy(bf16[20,5,128,128]{3,2,0,1:T(8,128)(2,1)} %fusion.17) | data formatting | bytes 6553600 | tf_op jit(solution)/shard_map/convert_element_type | solution.py:34
  342.5 9.2 %gather_fusion.1 = bf16[80,640,128]{2,1,0:T(8,128)(2,1)} fusion(bf16[20,640,128]{2,1,0:T(8,128)(2,1)} %bitcast.51, s32[1024]{0:T(1024)S(1)} %pad_clamp_fusion.4), kind=kCustom, calls=%fused_computation.3 | custom fusion | bytes 26214720 | tf_op jit(solution)/shard_map/jit(_take)/gather | solution.py:36
  351.7 8.9 %fusion.2 = f32[20,640,128,1]{1,2,3,0:T(8,128)} fusion(bf16[20,4,640,128]{3,2,1,0:T(8,128)(2,1)} %bitcast.58, pred[20,4]{1,0:T(8,128)(4,1)S(1)} %copy.43, bf16[1,20,4,128,128]{4,3,2,1,0:T(8,128)(2,1)S(1)} %copy-done), kind=kOutput, calls=%fused_computation.9 | convolution fusion | flops 1684275200 | bytes 22282320 | tf_op jit(solution)/shard_map/rkad,rkbd->rab/dot_general | solution.py:37
  360.6 8.2 %copy.55 = f32[1,640,2560]{2,1,0:T(8,128)} copy(f32[1,640,2560]{1,2,0:T(8,128)} %bitcast.60) | data formatting | bytes 13107200 | tf_op jit(solution)/shard_map/reshape | solution.py:64
  368.8 0.0 all-to-all-done.1
  368.8 9.2 %fusion.12 = bf16[1,640,2560]{2,1,0:T(8,128)(2,1)} fusion(f32[1,640,2560]{2,1,0:T(8,128)} %mul.23, f32[1,640,2560]{2,1,0:T(8,128)} %copy.55, bf16[1,640,2560]{2,1,0:T(8,128)(2,1)} %bitcast.49), kind=kLoop, calls=%fused_computation.21 | loop fusion | flops 6553600 | bytes 19660800 | tf_op jit(solution)/shard_map/convert_element_type | solution.py:69
  (30 shorter events, 0.1 us)
Async XLA Ops:
  6.5 327.5 %copy-start = (bf16[1,20,4,128,128]{4,3,2,1,0:T(8,128)(2,1)S(1)}, bf16[1,20,4,128,128]{4,3,2,1,0:T(8,128)(2,1)}, u32[]{:S(2)}) copy-start(bf16[1,20,4,128,128]{4,3,2,1,0:T(8,128)(2,1)} %param.11) | copy-start | bytes 7864324
  6.5 226.4 %all-gather.4.cloned.1.call-start = ((), (), s32[]{:S(2)}) async-start(), calls=%async_computation.2 | async-start | bytes 11796480 | tf_op jit(solution)/shard_map/all_gather | solution.py:51
  7.3 282.3 %all-gather.6.cloned.1.call-start = ((), (), s32[]{:S(2)}) async-start(), calls=%async_computation.3 | async-start | bytes 16384000 | tf_op jit(solution)/shard_map/all_gather | solution.py:26
  96.4 13.6 %copy-start.2 = (s32[80,4]{0,1:T(4,128)S(1)}, s32[80,4]{0,1:T(4,128)}, u32[]{:S(2)}) copy-start(s32[80,4]{0,1:T(4,128)} %param.14) | copy-start | bytes 3844
  96.4 14.0 %copy-start.4 = (s32[8]{0:T(128)S(1)}, s32[8]{0:T(128)}, u32[]{:S(2)}) copy-start(s32[8]{0:T(128)} %param.16) | copy-start | bytes 100
  96.4 14.8 %copy-start.5 = (s32[80]{0:T(128)S(1)}, s32[80]{0:T(128)}, u32[]{:S(2)}) copy-start(s32[80]{0:T(128)} %param.15) | copy-start | bytes 964
  103.6 80.0 %all-to-all-start = ((bf16[8,2,102400]{2,1,0:T(2,128)(2,1)}), bf16[8,2,102400]{2,1,0:T(2,128)(2,1)}, u32[]{:S(2)}, u32[]{:S(2)}) async-start(bf16[8,2,102400]{2,1,0:T(2,128)(2,1)} %reshape.190), calls=%async_computation | async-start | bytes 6553600 | tf_op jit(solution)/shard_map/all_to_all | solution.py:38
  267.4 9.3 %copy-start.3 = (s32[1,5,20]{2,0,1:T(1,128)S(1)}, s32[1,5,20]{2,0,1:T(1,128)}, u32[]{:S(2)}) copy-start(s32[1,5,20]{2,0,1:T(1,128)} %param.17) | copy-start | bytes 1204
  271.5 97.3 %all-to-all-start.1 = ((bf16[8,80,2560]{2,1,0:T(8,128)(2,1)}), bf16[8,80,2560]{2,1,0:T(8,128)(2,1)}, u32[]{:S(2)}, u32[]{:S(2)}) async-start(bf16[8,80,2560]{2,1,0:T(8,128)(2,1)} %broadcast_select_fusion), calls=%async_computation.1 | async-start | bytes 6553600 | tf_op jit(solution)/shard_map/all_to_all | solution.py:63
  280.3 8.6 %copy-start.1 = (s32[20,4]{0,1:T(4,128)S(1)}, s32[20,4]{0,1:T(4,128)}, u32[]{:S(2)}) copy-start(s32[20,4]{0,1:T(4,128)} %param.12) | copy-start | bytes 964
Sparse Core Ops, SparseCore 0:
  9.0 102.0 all-gather.3
  112.9 124.6 all-gather.5
where the time goes:
time: 387 us; the launch traced here: 385 us
  local copies, waits for them, and re-layouts  174 us (45%)
  other arithmetic  88.8 us (23%)
  waiting for transfers between devices  73.7 us (19%)
  matrix products  23.3 us (6%)
  between operations  13.6 us (4%)
  starting transfers between devices  11.6 us (3%)
    all_to_all x1, waiting for transfers between devices, on_device(): lax.all_to_all(amplitudes, 'pair', split_axis=1, concat_axis=0, tiled=True)  72.3 us
    unnamed x1, other arithmetic  71.4 us
    unnamed x17, local copies, waits for them, and re-layouts  37.4 us
    reshape x1, local copies, waits for them, and re-layouts, on_device(): gathered.reshape(tile_count, tile_size, tile_count, tile_size)  22.8 us
    gather x2, local copies, waits for them, and re-layouts, on_device(): jnp.take(gathered.reshape(tile_count, tile_size, tile_count, tile_size),...  21.7 us
    gather x1, local copies, waits for them, and re-layouts, on_device(): columns = jnp.take(left_tiles, cycle_tiles, axis=0)  13.8 us
    mul x2, local copies, waits for them, and re-layouts, on_device(): summed.reshape(local_tiles, tile_size, tile_count, tile_size) * mask_tiles  12.2 us
    gather x1, local copies, waits for them, and re-layouts, on_device(): integrals = jnp.take(slot_tiles, cycle_slots, axis=0)  10.1 us
  transfers between devices with their start and end apart: 4, of which 1 were waited for; matrix products, arithmetic and copies ran while one was open for 72% of the time, Pallas kernels for 0%

commit v1 on v0

--- a/solution.py
+++ b/solution.py
@@ -1,9 +1,361 @@
+import functools
+
 import jax
 import jax.numpy as jnp
 from jax import lax
+from jax.experimental import pallas as pl
+from jax.experimental.pallas import tpu as pltpu
 from jax.sharding import PartitionSpec as P
 
 NJ = 4
+CORES = 2
+MESH = pl.DeviceIdType.MESH
+
+
+def kernel(
+    pair_count,
+    vir_count,
+    ladder_tiles,
+    cycle_tiles,
+    cycle_slots,
+    slab_order,
+    inverse,
+    amplitudes,
+    amplitude_rows,
+    factor,
+    own_integrals,
+    mask_rows,
+    out,
+    pair_rows,
+    row_tiles,
+    integrals,
+    columns,
+    inner_out,
+    inner_in,
+    cycle_out,
+    cycle_in,
+    ladder_sum,
+    local_sem,
+    pair_sem,
+    back_sem,
+    vir_sem,
+    inner_sem,
+    near_sem,
+    share_sem,
+    core_sem,
+):
+    pair = lax.axis_index("pair")
+    vir = lax.axis_index("vir")
+    tile = factor.shape[-1]
+    kept = factor.shape[1]
+    kept_cycle = own_integrals.shape[1]
+    tile_count = factor.shape[0]
+    local_tiles = amplitudes.shape[0]
+    row_count = local_tiles * tile
+    sub_rows = pair_rows.shape[1]
+    own_slots = own_integrals.shape[0]
+    layer_count = pair_count // CORES
+    layer = pair // CORES
+    core = pair % CORES
+    other_core = layer * CORES + (1 - core)
+
+    def remote(src, dst, sems, index, device):
+        return pltpu.make_async_remote_copy(
+            src_ref=src,
+            dst_ref=dst,
+            send_sem=sems.at[0, index],
+            recv_sem=sems.at[1, index],
+            device_id=device,
+            device_id_type=MESH,
+        )
+
+    def rows_of(index):
+        return pl.ds(pl.multiple_of(index * sub_rows, 16), sub_rows)
+
+    def block_of(index):
+        return pl.ds(pl.multiple_of(index * row_count, tile), row_count)
+
+    def tile_at(index):
+        return pl.ds(pl.multiple_of(index * tile, tile), tile)
+
+    def slots_of(index):
+        return pl.ds(index * own_slots, own_slots)
+
+    def tiles_of(index):
+        return pl.ds(index * local_tiles, local_tiles)
+
+    barrier = pltpu.get_barrier_semaphore()
+    for step in range(1, pair_count):
+        pl.semaphore_signal(
+            barrier, inc=1, device_id={"pair": (pair + step) % pair_count}, device_id_type=MESH
+        )
+    for step in range(1, vir_count):
+        pl.semaphore_signal(
+            barrier, inc=1, device_id={"vir": (vir + step) % vir_count}, device_id_type=MESH
+        )
+    pl.semaphore_wait(barrier, pair_count + vir_count - 2)
+
+    near = []
+    for step in range(1, layer_count):
+        peer = ((layer + step) % layer_count) * CORES + core
+        copy = remote(
+            own_integrals.at[:, vir],
+            integrals.at[slots_of(pair), vir],
+            near_sem,
+            step,
+            {"pair": peer},
+        )
+        copy.start()
+        near.append(copy)
+    crossing = []
+    for step in range(1, vir_count):
+        peer = (vir + step) % vir_count
+        copy = remote(
+            amplitudes.at[:, :, block_of(peer)],
+            columns.at[tiles_of(vir)],
+            vir_sem,
+            step,
+            {"vir": peer},
+        )
+        copy.start()
+        crossing.append(copy)
+    order = sorted(range(1, pair_count), key=lambda step: -min(step, pair_count - step))
+    forward = []
+    for step in order:
+        peer = (pair + step) % pair_count
+        copy = remote(
+            amplitude_rows.at[rows_of(peer), :], pair_rows.at[pair], pair_sem, step, {"pair": peer}
+        )
+        copy.start()
+        forward.append(copy)
+    local = [
+        pltpu.make_async_copy(own_integrals, integrals.at[slots_of(pair)], local_sem.at[0]),
+        pltpu.make_async_copy(
+            amplitudes.at[:, :, block_of(vir)], columns.at[tiles_of(vir)], local_sem.at[1]
+        ),
+        pltpu.make_async_copy(
+            amplitude_rows.at[rows_of(pair), :], pair_rows.at[pair], local_sem.at[2]
+        ),
+    ]
+    for copy in local:
+        copy.start()
+    across = []
+    copy = remote(
+        own_integrals, integrals.at[slots_of(pair)], core_sem, 0, {"pair": other_core}
+    )
+    copy.start()
+    across.append(copy)
+
+    shared = []
+    for step in range(1, layer_count):
+        near[step - 1].wait_recv()
+        source = ((layer + layer_count - step) % layer_count) * CORES + core
+        for hop in range(1, vir_count):
+            copy = remote(
+                integrals.at[slots_of(source), vir],
+                integrals.at[slots_of(source), vir],
+                share_sem,
+                step * vir_count + hop,
+                {"vir": (vir + hop) % vir_count},
+            )
+            copy.start()
+            shared.append(copy)
+
+    for copy in crossing:
+        copy.wait_recv()
+    local[1].wait()
+
+    def inner_step(owner, index):
+        row_tile = owner * local_tiles + index
+        left = jnp.concatenate([factor[row_tile, k] for k in range(kept)], axis=1)
+        right = jnp.concatenate(
+            [columns[ladder_tiles[row_tile, k]] for k in range(kept)], axis=0
+        )
+        value = jnp.dot(left, right, preferred_element_type=jnp.float32).astype(jnp.bfloat16)
+        for part in range(local_tiles):
+            inner_out[owner, part, tile_at(index), :] = value[:, part * tile : (part + 1) * tile]
+
+    inner_sends = []
+    for step in list(range(1, vir_count)) + [0]:
+        peer = (vir + step) % vir_count
+
+        @pl.loop(0, local_tiles)
+        def _(index):
+            inner_step(peer, index)
+
+        if step:
+            copy = remote(
+                inner_out.at[peer], inner_in.at[tiles_of(vir)], inner_sem, step, {"vir": peer}
+            )
+            copy.start()
+            inner_sends.append(copy)
+        else:
+            own_inner = pltpu.make_async_copy(
+                inner_out.at[peer], inner_in.at[tiles_of(vir)], local_sem.at[3]
+            )
+            own_inner.start()
+
+    for step in range(1, layer_count):
+        for hop in range(1, vir_count):
+            shared[(step - 1) * (vir_count - 1) + hop - 1].wait_recv()
+        source = ((layer + layer_count - step) % layer_count) * CORES + core
+        copy = remote(
+            integrals.at[slots_of(source)],
+            integrals.at[slots_of(source)],
+            core_sem,
+            step,
+            {"pair": other_core},
+        )
+        copy.start()
+        across.append(copy)
+
+    def split_columns(source):
+        for index in range(tile_count):
+            row_tiles[source * tile_count + index] = pair_rows[
+                source, :, index * tile : (index + 1) * tile
+            ]
+
+    local[0].wait()
+    local[2].wait()
+    split_columns(pair)
+    for step, copy in zip(order, forward):
+        copy.wait_recv()
+        split_columns((pair + pair_count - step) % pair_count)
+    for copy in across:
+        copy.wait_recv()
+
+    def cycle_step(peer, index):
+        flat = slab_order[peer]
+        outer = lax.div(flat, NJ)
+        column = lax.rem(flat, NJ) * tile_count + index
+        pieces = []
+        for k in range(kept_cycle):
+            row_tile = cycle_tiles[column, k]
+            held = inverse[outer * NJ + lax.div(row_tile, tile_count)]
+            pieces.append(row_tiles[held * tile_count + lax.rem(row_tile, tile_count)])
+        left = jnp.concatenate(pieces, axis=1)
+        right = integrals[cycle_slots[column]].reshape(kept_cycle * tile, tile)
+        value = jnp.dot(left, right, preferred_element_type=jnp.float32)
+        cycle_out[peer, :, tile_at(index)] = value.astype(jnp.bfloat16)
+
+    back = []
+    for step in order + [0]:
+        peer = (pair + step) % pair_count
+
+        @pl.loop(0, tile_count)
+        def _(index):
+            cycle_step(peer, index)
+
+        if step:
+            copy = remote(
+                cycle_out.at[peer], cycle_in.at[rows_of(pair), :], back_sem, step, {"pair": peer}
+            )
+            copy.start()
+            back.append(copy)
+        else:
+            own_back = pltpu.make_async_copy(
+                cycle_out.at[peer], cycle_in.at[rows_of(pair), :], local_sem.at[4]
+            )
+            own_back.start()
+
+    for copy in inner_sends:
+        copy.wait_recv()
+    own_inner.wait()
+
+    @pl.loop(0, tile_count)
+    def _(index):
+        left = jnp.concatenate([inner_in[ladder_tiles[index, k]] for k in range(kept)], axis=1)
+        right = jnp.concatenate([factor[index, k] for k in range(kept)], axis=1)
+        ladder_sum[:, tile_at(index)] = lax.dot_general(
+            left, right, (((1,), (1,)), ((), ())), preferred_element_type=jnp.float32
+        )
+
+    def finish(source):
+        for part in range(sub_rows // 16):
+            row = source * sub_rows + part * 16
+            rows = pl.ds(pl.multiple_of(row, 16), 16)
+            total = ladder_sum[rows, :] + cycle_in[rows, :].astype(jnp.float32)
+            out[rows, :] = (mask_rows[pl.ds(row // tile, 1), :] * total).astype(jnp.bfloat16)
+
+    own_back.wait()
+    finish(pair)
+    for step, copy in sorted(zip(order, back), key=lambda item: item[0] not in (1, 7)):
+        copy.wait_recv()
+        finish((pair + pair_count - step) % pair_count)
+    for copy in near + crossing + forward + across + shared + inner_sends + back:
+        copy.wait_send()
+
+
+def fused(
+    amplitudes,
+    ladder_factor,
+    ladder_tiles,
+    cycle_integrals,
+    cycle_tiles,
+    cycle_slots,
+    slab_order,
+    amp_mask,
+    pair_count,
+    vir_count,
+):
+    tile = ladder_factor.shape[-1]
+    _, row_count, full_width = amplitudes.shape
+    tile_count = full_width // tile
+    sub_rows = row_count // pair_count
+    own_slots, kept_cycle = cycle_integrals.shape[:2]
+    positions = jnp.arange(pair_count, dtype=jnp.int32)
+    inverse = jnp.sum(
+        jnp.where(slab_order[None, :] == positions[:, None], positions[None, :], 0), axis=1
+    )
+    mask_rows = jnp.repeat(amp_mask[0].astype(jnp.float32), tile, axis=1)
+    smem = pl.BlockSpec(memory_space=pltpu.SMEM)
+    vmem = pl.BlockSpec(memory_space=pltpu.VMEM)
+    hbm = pl.BlockSpec(memory_space=pl.ANY)
+    layer_count = pair_count // CORES
+
+    def sems(count):
+        return pltpu.SemaphoreType.DMA((2, count))
+
+    result = pl.pallas_call(
+        functools.partial(kernel, pair_count, vir_count),
+        out_shape=jax.ShapeDtypeStruct((row_count, full_width), jnp.bfloat16),
+        in_specs=[smem] * 5 + [hbm, hbm, vmem, hbm, vmem],
+        out_specs=vmem,
+        scratch_shapes=[
+            pltpu.VMEM((pair_count, sub_rows, full_width), jnp.bfloat16),
+            pltpu.VMEM((pair_count * tile_count, sub_rows, tile), jnp.bfloat16),
+            pltpu.VMEM((own_slots * pair_count, kept_cycle, tile, tile), jnp.bfloat16),
+            pltpu.VMEM((tile_count, tile, row_count), jnp.bfloat16),
+            pltpu.VMEM((vir_count, row_count // tile, row_count, tile), jnp.bfloat16),
+            pltpu.VMEM((tile_count, row_count, tile), jnp.bfloat16),
+            pltpu.VMEM((pair_count, sub_rows, full_width), jnp.bfloat16),
+            pltpu.VMEM((row_count, full_width), jnp.bfloat16),
+            pltpu.VMEM((row_count, full_width), jnp.float32),
+            pltpu.SemaphoreType.DMA((5,)),
+            sems(pair_count),
+            sems(pair_count),
+            sems(vir_count),
+            sems(vir_count),
+            sems(layer_count),
+            sems(layer_count * vir_count),
+            sems(layer_count),
+        ],
+        compiler_params=pltpu.CompilerParams(
+            collective_id=0, has_side_effects=True, vmem_limit_bytes=56 * 1024 * 1024
+        ),
+    )(
+        ladder_tiles,
+        cycle_tiles,
+        cycle_slots,
+        slab_order,
+        inverse,
+        amplitudes.reshape(row_count // tile, tile, full_width),
+        amplitudes[0],
+        ladder_factor[0],
+        cycle_integrals,
+        mask_rows,
+    )
+    return result[None]
 
 
 def on_device(
@@ -80,8 +432,25 @@
         P("groups"),
         P(("groups", "pair"), "vir", None),
     )
+    pair_count, vir_count = mesh.shape["pair"], mesh.shape["vir"]
+
+    def per_device(*operands):
+        amplitudes, factor = operands[0], operands[1]
+        rows, width = amplitudes.shape[1:]
+        plain = (
+            amplitudes.shape[0] != 1
+            or factor.shape[0] != 1
+            or rows * vir_count != width
+            or rows % (16 * pair_count)
+            or pair_count % CORES
+            or operands[3].shape[1] != vir_count
+        )
+        if plain:
+            return on_device(*operands)
+        return fused(*operands, pair_count, vir_count)
+
     return jax.shard_map(
-        on_device,
+        per_device,
         mesh=mesh,
         in_specs=placed,
         out_specs=P(("groups", "pair"), "vir", None),

time: 387 us -> 190 us (0.49)
  Pallas kernels: 0 us -> 180 us
  local copies, waits for them, and re-layouts: 174 us -> 7.33 us
  other arithmetic: 88.8 us -> 2.03 us
  waiting for transfers between devices: 73.7 us -> 0 us
  matrix products: 23.3 us -> 0 us
  between operations: 13.6 us -> 0.01 us
  starting transfers between devices: 11.6 us -> 0 us
    pallas_call x0 -> x1, Pallas kernels: none -> 180 us  [fused(): pl.pallas_call(functools.partial(kernel, pair_count, vir_count), out_shap...]
    all_to_all x2 -> x0, waiting for transfers between devices: 72.3 us -> none  [the longest x1 72.3 us: on_device(): lax.all_to_all(amplitudes, 'pair', split_axis=1, concat_axis=0, tiled=True)]
    unnamed x1 -> x0, other arithmetic: 71.4 us -> none
    gather x7 -> x0, local copies, waits for them, and re-layouts: 63.6 us -> none  [the longest x2 21.7 us: on_device(): jnp.take(gathered.reshape(tile_count, tile_size, tile_count, tile_size),...]
    reshape x5 -> x0, local copies, waits for them, and re-layouts: 47.7 us -> none  [the longest x1 22.8 us: on_device(): gathered.reshape(tile_count, tile_size, tile_count, tile_size)]
    unnamed x17 -> x5, local copies, waits for them, and re-layouts: 37.4 us -> 7.33 us
    dot_general x3 -> x0, matrix products: 23.3 us -> none  [the longest x1 9.94 us: on_device(): jnp.einsum('tkrc,tkcb->trb', columns, integrals, preferred_element_type=j...]
    mul x2 -> x0, local copies, waits for them, and re-layouts: 12.2 us -> none  [on_device(): summed.reshape(local_tiles, tile_size, tile_count, tile_size) * mask_tiles]
  transfers between devices with their start and end apart: 4 -> 0, of which waited for: 1 -> 0; matrix products, arithmetic and copies ran while one was open for 72% -> 0% of each run, Pallas kernels for 0% -> 0%
where the time goes in v1:
time: 190 us
  Pallas kernels  180 us (95%)
  local copies, waits for them, and re-layouts  7.33 us (4%)
  other arithmetic  2.03 us (1%)
    pallas_call x1, Pallas kernels, fused(): pl.pallas_call(functools.partial(kernel, pair_count, vir_count), out_shap...  180 us
    unnamed x5, local copies, waits for them, and re-layouts  7.33 us

profile of v1, /device:TPU:1, one launch (start us, length us, event | category | flops | bytes accessed | tf_op | source)
XLA Modules:
  0.0 189.7 jit_solution(235662286676136472)
XLA Ops:
  0.0 1.3 select_reduce_fusion.inverse
  1.3 0.7 fusion
  2.0 1.4 copy.13.ladder_tiles
  3.4 1.4 copy.14.cycle_tiles
  4.8 0.1 broadcast_bitcast_fusion
  4.9 0.7 copy.20
  5.5 180.3 %shard_map.82 = bf16[640,2560]{1,0:T(8,128)(2,1)} custom-call(s32[20,4]{1,0:T(8,128)} %copy.13.ladder_tiles, s32[80,4]{1,0:T(8,128)} %copy.14.cycle_tiles, s32[80]{0:T(128)} %cycle_slots.1, s32[8]{0:T(128)} %slab_order.1, s32[8]{0:T(128)} %select_reduce_fusion.inverse, bf16[5,128,2560]{2,1,0:T(8,128)(2,1)} %bitcast.11, bf16[640,2560]{1,0:T(8,128)(2,1)} %bitcast.12, ...), custom_call_target="tpu_custom_call" | custom-call | tf_op jit(solution)/shard_map/pallas_call | solution.py:319
  185.8 3.8 %copy.22 = bf16[1,640,2560]{2,1,0:T(8,128)(2,1)} copy(bf16[1,640,2560]{2,1,0:T(8,128)(2,1)} %bitcast.13) | data formatting | bytes 6553600

commit v2 on v1

--- a/solution.py
+++ b/solution.py
@@ -9,6 +9,8 @@
 
 NJ = 4
 CORES = 2
+EARLY = 3
+BATCH = 2
 MESH = pl.DeviceIdType.MESH
 
 
@@ -19,13 +21,15 @@
     cycle_tiles,
     cycle_slots,
     slab_order,
-    inverse,
+    amp_mask,
     amplitudes,
     amplitude_rows,
     factor,
     own_integrals,
+    out,
+    finished,
     mask_rows,
-    out,
+    inverse,
     pair_rows,
     row_tiles,
     integrals,
@@ -43,6 +47,7 @@
     near_sem,
     share_sem,
     core_sem,
+    out_sem,
 ):
     pair = lax.axis_index("pair")
     vir = lax.axis_index("vir")
@@ -107,27 +112,12 @@
         )
         copy.start()
         near.append(copy)
-    crossing = []
-    for step in range(1, vir_count):
-        peer = (vir + step) % vir_count
-        copy = remote(
-            amplitudes.at[:, :, block_of(peer)],
-            columns.at[tiles_of(vir)],
-            vir_sem,
-            step,
-            {"vir": peer},
-        )
-        copy.start()
-        crossing.append(copy)
-    order = sorted(range(1, pair_count), key=lambda step: -min(step, pair_count - step))
-    forward = []
-    for step in order:
-        peer = (pair + step) % pair_count
-        copy = remote(
-            amplitude_rows.at[rows_of(peer), :], pair_rows.at[pair], pair_sem, step, {"pair": peer}
-        )
-        copy.start()
-        forward.append(copy)
+    across = []
+    copy = remote(
+        own_integrals, integrals.at[slots_of(pair)], core_sem, 0, {"pair": other_core}
+    )
+    copy.start()
+    across.append(copy)
     local = [
         pltpu.make_async_copy(own_integrals, integrals.at[slots_of(pair)], local_sem.at[0]),
         pltpu.make_async_copy(
@@ -139,27 +129,68 @@
     ]
     for copy in local:
         copy.start()
-    across = []
-    copy = remote(
-        own_integrals, integrals.at[slots_of(pair)], core_sem, 0, {"pair": other_core}
-    )
-    copy.start()
-    across.append(copy)
+
+    crossing = []
+    for step in range(1, vir_count):
+        peer = (vir + step) % vir_count
+        copy = remote(
+            amplitudes.at[:, :, block_of(peer)],
+            columns.at[tiles_of(vir)],
+            vir_sem,
+            step,
+            {"vir": peer},
+        )
+        crossing.append(copy)
+    order = sorted(range(1, pair_count), key=lambda step: -min(step, pair_count - step))
+    forward = []
+    for step in order:
+        peer = (pair + step) % pair_count
+        copy = remote(
+            amplitude_rows.at[rows_of(peer), :], pair_rows.at[pair], pair_sem, step, {"pair": peer}
+        )
+        forward.append(copy)
+    for copy in crossing[:EARLY]:
+        copy.start()
+
+    for flat in range(pair_count):
+        held = 0
+        for row in range(pair_count):
+            held = jnp.where(slab_order[row] == flat, row, held)
+        inverse[flat] = held
+    for row in range(local_tiles):
+        for index in range(tile_count):
+            mask_rows[row : row + 1, index * tile : (index + 1) * tile] = jnp.full(
+                (1, tile), amp_mask[row, index].astype(jnp.float32)
+            )
+
+    def source_of(step):
+        return ((layer + layer_count - step) % layer_count) * CORES + core
+
+    def share(source, kept_index, sems, index, device):
+        place = integrals.at[slots_of(source), kept_index]
+        copy = remote(place, place, sems, index, device)
+        copy.start()
+        return copy
 
     shared = []
     for step in range(1, layer_count):
         near[step - 1].wait_recv()
-        source = ((layer + layer_count - step) % layer_count) * CORES + core
+        source = source_of(step)
         for hop in range(1, vir_count):
-            copy = remote(
-                integrals.at[slots_of(source), vir],
-                integrals.at[slots_of(source), vir],
-                share_sem,
-                step * vir_count + hop,
-                {"vir": (vir + hop) % vir_count},
-            )
+            shared.append(
+                share(
+                    source,
+                    vir,
+                    share_sem,
+                    step * vir_count + hop,
+                    {"vir": (vir + hop) % vir_count},
+                )
+            )
+        across.append(share(source, vir, core_sem, step * vir_count, {"pair": other_core}))
+        for copy in forward[(step - 1) * BATCH : step * BATCH if step < layer_count - 1 else None]:
             copy.start()
-            shared.append(copy)
+    for copy in crossing[EARLY:]:
+        copy.start()
 
     for copy in crossing:
         copy.wait_recv()
@@ -169,7 +200,7 @@
         row_tile = owner * local_tiles + index
         left = jnp.concatenate([factor[row_tile, k] for k in range(kept)], axis=1)
         right = jnp.concatenate(
-            [columns[ladder_tiles[row_tile, k]] for k in range(kept)], axis=0
+            [columns[ladder_tiles[k, row_tile]] for k in range(kept)], axis=0
         )
         value = jnp.dot(left, right, preferred_element_type=jnp.float32).astype(jnp.bfloat16)
         for part in range(local_tiles):
@@ -198,16 +229,15 @@
     for step in range(1, layer_count):
         for hop in range(1, vir_count):
             shared[(step - 1) * (vir_count - 1) + hop - 1].wait_recv()
-        source = ((layer + layer_count - step) % layer_count) * CORES + core
-        copy = remote(
-            integrals.at[slots_of(source)],
-            integrals.at[slots_of(source)],
-            core_sem,
-            step,
-            {"pair": other_core},
-        )
-        copy.start()
-        across.append(copy)
+            across.append(
+                share(
+                    source_of(step),
+                    (vir + vir_count - hop) % vir_count,
+                    core_sem,
+                    step * vir_count + hop,
+                    {"pair": other_core},
+                )
+            )
 
     def split_columns(source):
         for index in range(tile_count):
@@ -230,7 +260,7 @@
         column = lax.rem(flat, NJ) * tile_count + index
         pieces = []
         for k in range(kept_cycle):
-            row_tile = cycle_tiles[column, k]
+            row_tile = cycle_tiles[k, column]
             held = inverse[outer * NJ + lax.div(row_tile, tile_count)]
             pieces.append(row_tiles[held * tile_count + lax.rem(row_tile, tile_count)])
         left = jnp.concatenate(pieces, axis=1)
@@ -264,24 +294,35 @@
 
     @pl.loop(0, tile_count)
     def _(index):
-        left = jnp.concatenate([inner_in[ladder_tiles[index, k]] for k in range(kept)], axis=1)
+        left = jnp.concatenate([inner_in[ladder_tiles[k, index]] for k in range(kept)], axis=1)
         right = jnp.concatenate([factor[index, k] for k in range(kept)], axis=1)
         ladder_sum[:, tile_at(index)] = lax.dot_general(
             left, right, (((1,), (1,)), ((), ())), preferred_element_type=jnp.float32
         )
+
+    stores = []
 
     def finish(source):
         for part in range(sub_rows // 16):
             row = source * sub_rows + part * 16
             rows = pl.ds(pl.multiple_of(row, 16), 16)
             total = ladder_sum[rows, :] + cycle_in[rows, :].astype(jnp.float32)
-            out[rows, :] = (mask_rows[pl.ds(row // tile, 1), :] * total).astype(jnp.bfloat16)
+            finished[rows, :] = (mask_rows[pl.ds(row // tile, 1), :] * total).astype(jnp.bfloat16)
+        copy = pltpu.make_async_copy(
+            finished.at[rows_of(source), :], out.at[rows_of(source), :], out_sem.at[len(stores)]
+        )
+        copy.start()
+        stores.append(copy)
 
     own_back.wait()
     finish(pair)
-    for step, copy in sorted(zip(order, back), key=lambda item: item[0] not in (1, 7)):
+    for step, copy in sorted(
+        zip(order, back), key=lambda item: item[0] not in (1, pair_count - 1)
+    ):
         copy.wait_recv()
         finish((pair + pair_count - step) % pair_count)
+    for copy in stores:
+        copy.wait()
     for copy in near + crossing + forward + across + shared + inner_sends + back:
         copy.wait_send()
 
@@ -303,11 +344,6 @@
     tile_count = full_width // tile
     sub_rows = row_count // pair_count
     own_slots, kept_cycle = cycle_integrals.shape[:2]
-    positions = jnp.arange(pair_count, dtype=jnp.int32)
-    inverse = jnp.sum(
-        jnp.where(slab_order[None, :] == positions[:, None], positions[None, :], 0), axis=1
-    )
-    mask_rows = jnp.repeat(amp_mask[0].astype(jnp.float32), tile, axis=1)
     smem = pl.BlockSpec(memory_space=pltpu.SMEM)
     vmem = pl.BlockSpec(memory_space=pltpu.VMEM)
     hbm = pl.BlockSpec(memory_space=pl.ANY)
@@ -319,9 +355,12 @@
     result = pl.pallas_call(
         functools.partial(kernel, pair_count, vir_count),
         out_shape=jax.ShapeDtypeStruct((row_count, full_width), jnp.bfloat16),
-        in_specs=[smem] * 5 + [hbm, hbm, vmem, hbm, vmem],
-        out_specs=vmem,
+        in_specs=[smem] * 5 + [hbm, hbm, vmem, hbm],
+        out_specs=hbm,
         scratch_shapes=[
+            pltpu.VMEM((row_count, full_width), jnp.bfloat16),
+            pltpu.VMEM((row_count // tile, full_width), jnp.float32),
+            pltpu.SMEM((pair_count,), jnp.int32),
             pltpu.VMEM((pair_count, sub_rows, full_width), jnp.bfloat16),
             pltpu.VMEM((pair_count * tile_count, sub_rows, tile), jnp.bfloat16),
             pltpu.VMEM((own_slots * pair_count, kept_cycle, tile, tile), jnp.bfloat16),
@@ -338,22 +377,22 @@
             sems(vir_count),
             sems(layer_count),
             sems(layer_count * vir_count),
-            sems(layer_count),
+            sems(layer_count * vir_count),
+            pltpu.SemaphoreType.DMA((pair_count,)),
         ],
         compiler_params=pltpu.CompilerParams(
             collective_id=0, has_side_effects=True, vmem_limit_bytes=56 * 1024 * 1024
         ),
     )(
-        ladder_tiles,
-        cycle_tiles,
+        ladder_tiles.T,
+        cycle_tiles.T,
         cycle_slots,
         slab_order,
-        inverse,
+        amp_mask[0],
         amplitudes.reshape(row_count // tile, tile, full_width),
         amplitudes[0],
         ladder_factor[0],
         cycle_integrals,
-        mask_rows,
     )
     return result[None]
 

time: 190 us -> 185 us (0.974)
  local copies, waits for them, and re-layouts: 7.33 us -> 5.12 us
  other arithmetic: 2.03 us -> 0 us
    unnamed x5 -> x2, local copies, waits for them, and re-layouts: 7.33 us -> 5.12 us
where the time goes in v2:
time: 185 us
  Pallas kernels  180 us (97%)
  local copies, waits for them, and re-layouts  5.12 us (3%)
    pallas_call x1, Pallas kernels, fused(): pl.pallas_call(functools.partial(kernel, pair_count, vir_count), out_shap...  180 us
    unnamed x2, local copies, waits for them, and re-layouts  5.12 us

profile of v2, /device:TPU:1, one launch (start us, length us, event | category | flops | bytes accessed | tf_op | source)
XLA Modules:
  0.0 184.9 jit_solution(13356996349035664308)
XLA Ops:
  0.0 1.3 copy.11
  1.3 179.8 %shard_map.82 = bf16[640,2560]{1,0:T(8,128)(2,1)} custom-call(s32[4,20]{1,0:T(4,128)} %bitcast.14, s32[4,80]{1,0:T(4,128)} %bitcast.15, s32[80]{0:T(128)} %cycle_slots.1, s32[8]{0:T(128)} %slab_order.1, s32[5,20]{1,0:T(8,128)} %bitcast.13, bf16[5,128,2560]{2,1,0:T(8,128)(2,1)} %bitcast.9, bf16[640,2560]{1,0:T(8,128)(2,1)} %bitcast.10, ...), custom_call_target="tpu_custom_call" | custom-call | tf_op jit(solution)/shard_map/pallas_call | solution.py:355
  181.1 3.8 %copy.13 = bf16[1,640,2560]{2,1,0:T(8,128)(2,1)} copy(bf16[1,640,2560]{2,1,0:T(8,128)(2,1)} %bitcast.11) | data formatting | bytes 6553600
